TPU v7x, 32 devices: a whole 2x2x4 slice. The times are simulated.
32 devices in a mesh: wide: 8 (over z, y), sub: 4 (over x, core).
Axes of the slice: x: 2, y: 2, z: 4, core: 2. Of those that a mesh axis runs over, the one named last changes fastest.
Arguments:
- lengths: int32 [4, 1024], P('sub', 'wide'), may hold values from 0 to 2048, as said below
- postings: bfloat16 [4, 16384, 128], P('sub', 'wide'), may hold values from -6 to 6
- codes: int32 [4, 8, 16384], P('sub', None, 'wide'), may hold values from 0 to 255
- rotation: bfloat16 [128, 128], replicated, may hold values from -0.5 to 0.5
Outputs:
- rotated_slices: bfloat16 [4, 128, 8192], P(None, 'sub', 'wide')
- codebook: float32 [8, 16, 256], P('sub')
Inputs may be any that keep to these rules, and one draw needn't show every extreme that they name: Each slab's lengths add up to 8192; no device holds more than 2048 rows in all; in each slab some device holds exactly 2048 rows, all in one list; lengths and whole devices may be empty.
All inputs are finite; a program needn't handle non-finite values.
Results may differ from a plain program's by a relative error of at most 0.0029.
Values may be sent and summed in bfloat16 or wider, within the bound.
A program may use at most 128 MiB of HBM per device.

v0:
```python
import jax
import jax.numpy as jnp
from jax import lax
from jax.sharding import PartitionSpec as P

KCODES = 256
SUBDIM = 16


def entering(part, axis, combine, identity):
    place = lax.axis_index(axis)
    gathered = lax.all_gather(part, axis)
    state = jnp.zeros_like(part) + jnp.asarray(identity, part.dtype)

    def one(turn, state):
        return combine(state, lax.dynamic_index_in_dim(gathered, turn, 0, False))

    return lax.fori_loop(0, place, one, state)


def add_counts(earlier, later):
    return earlier + later


def body(lengths, postings, codes, rotation):
    here = lax.axis_index("wide")
    capacity = postings.shape[1]
    per_shard = capacity // 2
    total = jnp.sum(lengths)
    offset = entering(total, "wide", add_counts, jnp.int32(0))
    marks = jnp.stack([offset, total]).astype(jnp.int32).reshape(1, 1, 2)
    code_rows = jnp.swapaxes(codes, 1, 2)
    targets = here * per_shard + jnp.arange(per_shard, dtype=jnp.int32)

    def place(carry, pieces, start):
        rows_piece, code_piece, mark_piece = pieces
        shards = mark_piece.shape[1]
        slots = rows_piece.shape[1] // shards

        def one_shard(shard, state):
            rows_acc, code_acc = state
            block_rows = lax.dynamic_slice_in_dim(rows_piece[0], shard * slots, slots, 0)
            block_codes = lax.dynamic_slice_in_dim(code_piece[0], shard * slots, slots, 0)
            source_start = mark_piece[0, shard, 0]
            source_total = mark_piece[0, shard, 1]
            within = targets - source_start
            usable = (within >= 0) & (within < source_total)
            safe = jnp.clip(within, 0, slots - 1)
            rows_acc = jnp.where(usable[:, None], jnp.take(block_rows, safe, axis=0), rows_acc)
            code_acc = jnp.where(usable[:, None], jnp.take(block_codes, safe, axis=0), code_acc)
            return (rows_acc, code_acc)

        return lax.fori_loop(0, shards, one_shard, carry)

    start_rows = jnp.zeros((per_shard, postings.shape[2]), jnp.bfloat16)
    start_codes = jnp.zeros((per_shard, codes.shape[1]), jnp.int32)
    kept, kept_code_rows = place(
        (start_rows, start_codes),
        (
            lax.all_gather(postings, "wide", axis=1, tiled=True),
            lax.all_gather(code_rows, "wide", axis=1, tiled=True),
            lax.all_gather(marks, "wide", axis=1, tiled=True),
        ),
        jnp.int32(0),
    )
    kept_codes = kept_code_rows.T
    rotated = jnp.einsum("rd,de->er", kept, rotation, preferred_element_type=jnp.float32).astype(
        jnp.bfloat16
    )
    slices, slice_codes = (
        lax.all_to_all(rotated[None], "sub", split_axis=1, concat_axis=0, tiled=True),
        lax.all_to_all(kept_codes[None], "sub", split_axis=1, concat_axis=0, tiled=True),
    )
    local_count = slice_codes.shape[1]
    centroid_ids = jnp.arange(KCODES, dtype=jnp.int32)
    sum_list = []
    count_list = []
    for local in range(local_count):
        values = slices[:, local * SUBDIM : (local + 1) * SUBDIM, :]
        onehot = (slice_codes[:, local, :, None] == centroid_ids).astype(jnp.bfloat16)
        sum_list.append(
            jnp.einsum("gde,gek->dk", values, onehot, preferred_element_type=jnp.float32)
        )
        count_list.append(jnp.sum(onehot.astype(jnp.float32), axis=(0, 1)))
    partial_sums = jnp.stack(sum_list)
    partial_counts = jnp.stack(count_list)
    full_sums, full_counts = lax.psum((partial_sums, partial_counts), "wide")
    codebook = full_sums / (full_counts[:, None, :] + 1.0)
    return (slices, codebook)


def solution(mesh):
    return jax.shard_map(
        body,
        mesh=mesh,
        in_specs=(P("sub", "wide"), P("sub", "wide", None), P("sub", None, "wide"), P()),
        out_specs=(P(None, "sub", "wide"), P("sub", None, None)),
        check_vma=False,
    )
```

profile of v0, /device:TPU:0, one launch (start us, length us, event | category | flops | bytes accessed | tf_op | source)
XLA Modules:
  0.0 384.8 jit_solution(17787069196864160257)
XLA Ops:
  7.2 0.7 all-gather.3.cloned.1.call-update
  7.9 1.2 dynamic-slice.6
  9.2 1.3 reduce_sum.27
  10.5 1.4 dynamic-update-slice
  11.9 13.2 %all-reduce = s32[8]{0:T(128)S(1)} all-reduce(s32[8]{0:T(128)S(1)} %dynamic-update-slice), channel_id=1, replica_groups=mesh['wide'=8,'sub'=4] {'wide'}, use_global_device_ids=true, to_apply=%add | all-reduce | flops 8 | bytes 64
  25.7 0.8 add_dynamic-update-slice_fusion
  26.5 15.9 %all-reduce.1 = s32[16]{0:T(128)S(1)} all-reduce(s32[16]{0:T(128)S(1)} %add_dynamic-update-slice_fusion), channel_id=2, replica_groups=mesh['wide'=8,'sub'=4] {'wide'}, use_global_device_ids=true, to_apply=%add.1 | all-reduce | flops 16 | bytes 128
  42.6 1.2 copy.17
  43.8 179.0 %all_gather.19 = s32[1,16384,8]{2,1,0:T(8,128)} all-gather(s32[1,2048,8]{2,1,0:T(8,128)S(1)} %bitcast.50), channel_id=1, replica_groups=mesh['wide'=8,'sub'=4] {'wide'}, dimensions={1}, use_global_device_ids=true | all-gather | bytes 589824 | tf_op jit(solution)/shard_map/all_gather | solution.py:61
  222.8 96.4 %while.27 = (s32[]{:T(128)}, bf16[1024,128]{1,0:T(8,128)(2,1)S(1)}, s32[1024,8]{1,0:T(8,128)S(1)}, s32[1,8,2]{1,2,0:T(2,128)S(1)}, bf16[1,16384,128]{2,1,0:T(8,1...) while((s32[]{:T(128)}, bf16[1024,128]{1,0:T(8,128)(2,1)S(1)}, ...), condition=%wide.region_4.5_spmd.clone, body=%wide.region_3.4_spmd.clone.sunk | while | flops 437255 | bytes 2689238 | solution.py:53
  222.8 1.3 dynamic-slice_bitcast_fusion.5
  224.7 0.7 fusion.22
  225.4 2.8 gather_fusion.1
  228.3 1.3 fusion.23
  230.0 1.1 dynamic-slice_bitcast_fusion.4
  231.1 3.2 gather_fusion
  234.8 1.3 dynamic-slice_bitcast_fusion.5
  236.8 0.7 fusion.22
  237.5 2.8 gather_fusion.1
  240.3 1.3 fusion.23
  242.1 1.1 dynamic-slice_bitcast_fusion.4
  243.2 3.2 gather_fusion
  246.9 1.3 dynamic-slice_bitcast_fusion.5
  248.8 0.7 fusion.22
  249.5 2.8 gather_fusion.1
  252.4 1.3 fusion.23
  254.1 1.1 dynamic-slice_bitcast_fusion.4
  255.2 3.2 gather_fusion
  258.9 1.3 dynamic-slice_bitcast_fusion.5
  261.6 2.8 gather_fusion.1
  264.4 1.3 fusion.23
  266.2 1.1 dynamic-slice_bitcast_fusion.4
  267.3 3.2 gather_fusion
  271.0 1.3 dynamic-slice_bitcast_fusion.5
  273.6 2.8 gather_fusion.1
  276.5 1.3 fusion.23
  278.2 1.1 dynamic-slice_bitcast_fusion.4
  279.3 3.2 gather_fusion
  283.0 1.3 dynamic-slice_bitcast_fusion.5
  285.7 2.8 gather_fusion.1
  288.5 1.3 fusion.23
  290.3 1.1 dynamic-slice_bitcast_fusion.4
  291.4 3.2 gather_fusion
  295.1 1.3 dynamic-slice_bitcast_fusion.5
  297.0 0.7 fusion.22
  297.7 2.8 gather_fusion.1
  300.6 1.3 fusion.23
  302.3 1.1 dynamic-slice_bitcast_fusion.4
  303.4 3.2 gather_fusion
  307.1 1.3 dynamic-slice_bitcast_fusion.5
  309.8 2.8 gather_fusion.1
  312.6 1.3 fusion.23
  314.4 1.1 dynamic-slice_bitcast_fusion.4
  315.5 3.2 gather_fusion
  320.0 3.3 all-to-all-start.1
  324.5 2.1 reduce.1
  326.6 0.9 reshape.97
  327.5 3.4 all-to-all-start
  331.1 0.8 convert_reduce_fusion.1
  331.9 0.8 convert_reduce_fusion
  332.7 4.2 %all-to-all-done = bf16[4,2,16384]{2,1,0:T(2,128)(2,1)S(1)} async-done(((bf16[4,2,16384]{2,1,0:T(2,128)(2,1)}), bf16[4,2,16384]{2,1,0:T(2,128)(2,1)S(1)}, u32[]{:S(2)}, u32[]{:S(2)}) %all-to-all-start) | async-done | bytes 262176 | tf_op jit(solution)/shard_map/all_to_all | solution.py:71
  337.3 1.4 fusion.13
  338.7 1.4 fusion.14
  340.1 37.2 %all-reduce.2 = (f32[2,16,256]{2,1,0:T(8,128)S(1)}, f32[2,256]{1,0:T(2,128)S(1)}) all-reduce(f32[2,16,256]{2,1,0:T(8,128)S(1)} %pad_maximum_fusion, f32[2,256]{1,0:T(2,128)S(1)} %pad_maximum_fusion.1), channel_id=1, replica_groups=mesh['wide'=8,'sub'=4] {'wide'}, use_global_device_ids=true, to_apply=%region_5.6 | all-reduce | flops 8704 | bytes 69632 | tf_op jit(solution)/shard_map/psum | solution.py:87
  (73 shorter events, 19.0 us)
Async XLA Ops:
  7.2 316.1 %copy-start = (bf16[128,128]{1,0:T(8,128)(2,1)S(1)}, bf16[128,128]{1,0:T(8,128)(2,1)}, u32[]{:S(2)}) copy-start(bf16[128,128]{1,0:T(8,128)(2,1)} %param.11) | copy-start | bytes 98308
  7.2 215.6 %all-gather.3.cloned.1.call-start = ((), (), s32[]{:S(2)}) async-start(), calls=%async_computation.2 | async-start | bytes 4718592 | tf_op jit(solution)/shard_map/all_gather | solution.py:60
  320.0 7.6 %all-to-all-start.1 = ((s32[1,8,1024]{2,0,1:T(1,128)}), s32[1,8,1024]{2,0,1:T(1,128)S(1)}, u32[]{:S(2)}, u32[]{:S(2)}) async-start(s32[1,8,1024]{2,0,1:T(1,128)} %broadcast_in_dim.90), calls=%async_computation.1 | async-start | bytes 65536 | tf_op jit(solution)/shard_map/all_to_all | solution.py:72
  327.5 9.4 %all-to-all-start = ((bf16[4,2,16384]{2,1,0:T(2,128)(2,1)}), bf16[4,2,16384]{2,1,0:T(2,128)(2,1)S(1)}, u32[]{:S(2)}, u32[]{:S(2)}) async-start(bf16[4,2,16384]{2,1,0:T(2,128)(2,1)} %reshape.97), calls=%async_computation | async-start | bytes 524288 | tf_op jit(solution)/shard_map/all_to_all | solution.py:71
  337.3 40.7 %copy-start.1 = (bf16[1,128,1024]{2,1,0:T(8,128)(2,1)}, bf16[1,128,1024]{2,1,0:T(8,128)(2,1)S(1)}, u32[]{:S(2)}) copy-start(bf16[1,128,1024]{2,1,0:T(8,128)(2,1)S(1)} %copy.21) | copy-start | bytes 786436
Sparse Core Ops, SparseCore 0:
  10.1 137.8 all-gather.2
where the time goes:
time: 386 us; the launch traced here: 385 us
  blocking collectives  245 us (63%)
  local copies, waits for them, and re-layouts  79.5 us (21%)
  other arithmetic  30 us (8%)
  between operations  14.8 us (4%)
  starting transfers between devices  6.71 us (2%)
  waiting for transfers between devices  4.89 us (1%)
    all_gather x1, blocking collectives, body(): lax.all_gather(code_rows, 'wide', axis=1, tiled=True)  179 us
    psum x1, blocking collectives, body(): full_sums, full_counts = lax.psum((partial_sums, partial_counts), 'wide')  37.2 us
    unnamed x2, blocking collectives  29.1 us
    gather x8, local copies, waits for them, and re-layouts, one_shard(): jnp.take(block_rows, safe, axis=0)  25.6 us
    gather x8, local copies, waits for them, and re-layouts, one_shard(): jnp.take(block_codes, safe, axis=0)  22.5 us
    dynamic_slice x8, local copies, waits for them, and re-layouts, one_shard(): lax.dynamic_slice_in_dim(code_piece[0], shard * slots, slots, 0)  10.4 us
    and x8, other arithmetic, one_shard(): usable = (within >= 0) & (within < source_total)  10.3 us
    dynamic_slice x8, local copies, waits for them, and re-layouts, one_shard(): lax.dynamic_slice_in_dim(rows_piece[0], shard * slots, slots, 0)  8.67 us
  transfers between devices with their start and end apart: 3, of which 1 were waited for; matrix products, arithmetic and copies ran while one was open for 3% of the time, Pallas kernels for 0%

commit v1 on v0

--- a/solution.py
+++ b/solution.py
@@ -1,3 +1,4 @@
+import functools
 import jax
 import jax.numpy as jnp
 from jax import lax
@@ -5,6 +6,34 @@
 
 KCODES = 256
 SUBDIM = 16
+
+
+def solve_threads_on(w_in, mesh_dim):
+    finding = lax.axis_size(mesh_dim)
+    part_now = lax.axis_index(mesh_dim)
+    next_value, odd, far_arr = (finding, part_now, w_in.shape[1])
+    reached = map(lambda s: (s, (s + 1) % next_value), range(next_value))
+    so_far_all = list(reached)
+    high = map(lambda s: (s, (s - 1) % next_value), range(next_value))
+    copies = list(high)
+    last = jnp.zeros((*w_in.shape[:1], next_value * far_arr, *w_in.shape[2:]), w_in.dtype)
+    last = lax.dynamic_update_slice_in_dim(last, w_in, odd * far_arr, axis=1)
+    long_array = all_rows = w_in
+    val = next_value // 2
+    for tick in range(1, val + 1):
+        long_array = lax.ppermute(long_array, mesh_dim, so_far_all)
+        last = lax.dynamic_update_slice_in_dim(
+            last, long_array, (odd - tick) % next_value * far_arr, axis=1
+        )
+        if tick < next_value - val:
+            all_rows = lax.ppermute(all_rows, mesh_dim, copies)
+            last = lax.dynamic_update_slice_in_dim(
+                last, all_rows, (odd + tick) % next_value * far_arr, axis=1
+            )
+    return last
+
+
+slots_close = functools.partial(solve_threads_on, mesh_dim="wide")
 
 
 def entering(part, axis, combine, identity):
@@ -58,7 +87,7 @@
         (start_rows, start_codes),
         (
             lax.all_gather(postings, "wide", axis=1, tiled=True),
-            lax.all_gather(code_rows, "wide", axis=1, tiled=True),
+            slots_close(code_rows),
             lax.all_gather(marks, "wide", axis=1, tiled=True),
         ),
         jnp.int32(0),

time: 386 us -> 254 us (0.66)
  blocking collectives: 245 us -> 63.2 us
  waiting for transfers between devices: 4.89 us -> 25 us
  starting transfers between devices: 6.71 us -> 22.5 us
  local copies, waits for them, and re-layouts: 79.5 us -> 93.8 us
    all_gather x1 -> x0, blocking collectives: 179 us -> none  [body(): lax.all_gather(code_rows, 'wide', axis=1, tiled=True)]
    ppermute x0 -> x7, starting transfers between devices: none -> 15.8 us  [the longest x3 11.3 us: solve_threads_on(): all_rows = lax.ppermute(all_rows, mesh_dim, copies)]
    all_gather x1, waiting for transfers between devices: 0.01 us -> 12.5 us  [body(): lax.all_gather(postings, 'wide', axis=1, tiled=True)]
    dynamic_update_slice x0 -> x8, local copies, waits for them, and re-layouts: none -> 8.51 us  [the longest x4 4.25 us: solve_threads_on(): lax.dynamic_update_slice_in_dim(last, long_array, (odd - tick) % next_val...]
    ppermute x0 -> x7, waiting for transfers between devices: none -> 7.62 us  [the longest x4 7.62 us: solve_threads_on(): long_array = lax.ppermute(long_array, mesh_dim, so_far_all)]
  transfers between devices with their start and end apart: 3 -> 10, of which waited for: 1 -> 5; matrix products, arithmetic and copies ran while one was open for 3% -> 10% of each run, Pallas kernels for 0% -> 0%
where the time goes in v1:
time: 254 us; the launch traced here: 253 us
  local copies, waits for them, and re-layouts  93.8 us (37%)
  blocking collectives  63.2 us (25%)
  other arithmetic  30 us (12%)
  waiting for transfers between devices  25 us (10%)
  starting transfers between devices  22.5 us (9%)
  between operations  14.9 us (6%)
  matrix products  2.98 us (1%)
    psum x1, blocking collectives, body(): full_sums, full_counts = lax.psum((partial_sums, partial_counts), 'wide')  34.7 us
    unnamed x2, blocking collectives  28.5 us
    gather x8, local copies, waits for them, and re-layouts, one_shard(): jnp.take(block_rows, safe, axis=0)  25.6 us
    gather x8, local copies, waits for them, and re-layouts, one_shard(): jnp.take(block_codes, safe, axis=0)  22.5 us
    all_gather x1, waiting for transfers between devices, body(): lax.all_gather(postings, 'wide', axis=1, tiled=True)  12.5 us
    ppermute x3, starting transfers between devices, solve_threads_on(): all_rows = lax.ppermute(all_rows, mesh_dim, copies)  11.3 us
    dynamic_slice x8, local copies, waits for them, and re-layouts, one_shard(): lax.dynamic_slice_in_dim(code_piece[0], shard * slots, slots, 0)  10.4 us
    and x8, other arithmetic, one_shard(): usable = (within >= 0) & (within < source_total)  10.3 us
  transfers between devices with their start and end apart: 10, of which 5 were waited for; matrix products, arithmetic and copies ran while one was open for 10% of the time, Pallas kernels for 0%

profile of v1, /device:TPU:0, one launch (start us, length us, event | category | flops | bytes accessed | tf_op | source)
XLA Modules:
  0.0 253.1 jit_solution(4811425691137207825)
XLA Ops:
  7.9 3.0 %collective-permute-start = (s32[1,2048,8]{1,2,0:T(8,128)}, s32[1,2048,8]{1,2,0:T(8,128)S(1)}, u32[]{:S(2)}, u32[]{:S(2)}) collective-permute-start(s32[1,2048,8]{1,2,0:T(8,128)} %bitcast.58), channel_id=1, source_target_pairs={{0,4},{4,8},{8,12},{12,16},{16,20},{20,24},{24,28},{28,0},{1,5},{5... | collective-permute-start | bytes 196616 | tf_op jit(solution)/shard_map/ppermute | solution.py:24
  10.9 1.2 dynamic-slice.6
  12.2 1.3 reduce_sum.27
  13.5 1.4 dynamic-update-slice
  14.9 3.1 %collective-permute-start.1 = (s32[1,2048,8]{1,2,0:T(8,128)}, s32[1,2048,8]{1,2,0:T(8,128)S(1)}, u32[]{:S(2)}, u32[]{:S(2)}) collective-permute-start(s32[1,2048,8]{1,2,0:T(8,128)} %bitcast.59), channel_id=1, source_target_pairs={{0,28},{4,0},{8,4},{12,8},{16,12},{20,16},{24,20},{28,24},{1,29},{... | collective-permute-start | bytes 196616 | tf_op jit(solution)/shard_map/ppermute | solution.py:29
  17.9 10.1 %all-reduce = s32[8]{0:T(128)S(1)} all-reduce(s32[8]{0:T(128)S(1)} %dynamic-update-slice), channel_id=1, replica_groups=mesh['wide'=8,'sub'=4] {'wide'}, use_global_device_ids=true, to_apply=%add | all-reduce | flops 8 | bytes 64
  28.0 1.2 copy.17
  30.7 3.5 %broadcast_in_dim.92 = s32[1,16384,8]{2,1,0:T(8,128)} broadcast(s32[]{:T(128)} %constant.146.clone.1), dimensions={} | broadcast | bytes 524292 | tf_op jit(solution)/shard_map/broadcast_in_dim | solution.py:19
  35.3 18.4 %all-reduce.1 = s32[16]{0:T(128)S(1)} all-reduce(s32[16]{0:T(128)S(1)} %add_dynamic-update-slice_fusion), channel_id=2, replica_groups=mesh['wide'=8,'sub'=4] {'wide'}, use_global_device_ids=true, to_apply=%add.1 | all-reduce | flops 16 | bytes 128
  54.2 1.4 collective-permute-start.2
  55.9 3.5 %collective-permute-start.3 = (s32[1,2048,8]{1,2,0:T(8,128)S(1)}, s32[1,2048,8]{1,2,0:T(8,128)S(1)}, u32[]{:S(2)}, u32[]{:S(2)}) collective-permute-start(s32[1,2048,8]{1,2,0:T(8,128)S(1)} %collective-permute-done.1), channel_id=1, source_target_pairs={{0,28},{4,0},{8,4},{12,8},{16,12},{20,16},{24,20},{28,24},{1,29},{... | collective-permute-start | bytes 196616 | tf_op jit(solution)/shard_map/ppermute | solution.py:29
  60.4 1.1 constant_dynamic-update-slice_fusion.5
  61.5 1.6 collective-permute-done.2
  63.9 4.8 %collective-permute-start.5 = (s32[1,2048,8]{1,2,0:T(8,128)S(1)}, s32[1,2048,8]{1,2,0:T(8,128)S(1)}, u32[]{:S(2)}, u32[]{:S(2)}) collective-permute-start(s32[1,2048,8]{1,2,0:T(8,128)S(1)} %collective-permute-done.3), channel_id=1, source_target_pairs={{0,28},{4,0},{8,4},{12,8},{16,12},{20,16},{24,20},{28,24},{1,29},{... | collective-permute-start | bytes 196616 | tf_op jit(solution)/shard_map/ppermute | solution.py:29
  70.8 1.5 collective-permute-done.4
  73.1 1.1 constant_dynamic-update-slice_fusion.2
  75.2 4.5 %collective-permute-done.6 = s32[1,2048,8]{1,2,0:T(8,128)S(1)} collective-permute-done((s32[1,2048,8]{1,2,0:T(8,128)S(1)}, s32[1,2048,8]{1,2,0:T(8,128)S(1)}, u32[]{:S(2)}, u32[]{:S(2)}) %collective-permute-start.6) | collective-permute-done | bytes 65568 | tf_op jit(solution)/shard_map/ppermute | solution.py:24
  81.0 12.5 %all-gather.3.cloned.1.call-done = bf16[1,16384,128]{2,1,0:T(8,128)(2,1)} async-done(((bf16[1,2048,128]{2,1,0:T(8,128)(2,1)}), bf16[1,16384,128]{2,1,0:T(8,128)(2,1)}) %all-gather.3.cloned.1.call-update) | async-done | bytes 4194320 | tf_op jit(solution)/shard_map/all_gather | solution.py:89
  93.5 96.4 %while.27 = (s32[]{:T(128)}, bf16[1024,128]{1,0:T(8,128)(2,1)S(1)}, s32[1024,8]{1,0:T(8,128)S(1)}, s32[1,8,2]{1,2,0:T(2,128)S(1)}, bf16[1,16384,128]{2,1,0:T(8,1...) while((s32[]{:T(128)}, bf16[1024,128]{1,0:T(8,128)(2,1)S(1)}, ...), condition=%wide.region_4.5_spmd.clone, body=%wide.region_3.4_spmd.clone.sunk | while | flops 437255 | bytes 2689238 | solution.py:82
  93.5 1.3 dynamic-slice_bitcast_fusion.5
  96.2 2.8 %gather_fusion.1 = s32[1024,8]{1,0:T(8,128)S(1)} fusion(s32[2048,8]{1,0:T(8,128)S(1)} %dynamic-slice_bitcast_fusion.5, s32[1024]{0:T(1024)S(1)} %broadcast_clamp_fusion.2), kind=kCustom, calls=%fused_computation.1.clone.clone.1 | custom fusion | bytes 69632 | tf_op jit(solution)/shard_map/while/body/eval_jaxpr/jit(_take)/gather | solution.py:79
  99.0 1.3 fusion.23
  100.8 1.1 dynamic-slice_bitcast_fusion.4
  101.9 3.2 %gather_fusion = bf16[1024,128]{1,0:T(8,128)(2,1)S(1)} fusion(bf16[2048,128]{1,0:T(8,128)(2,1)S(1)} %dynamic-slice_bitcast_fusion.4, s32[1024]{0:T(1024)S(1)} %broadcast_clamp_fusion.2), kind=kCustom, calls=%fused_computation.clone.clone.1 | custom fusion | bytes 528384 | tf_op jit(solution)/shard_map/while/body/eval_jaxpr/jit(_take)/gather | solution.py:78
  105.6 1.3 dynamic-slice_bitcast_fusion.5
  108.2 2.8 %gather_fusion.1 = s32[1024,8]{1,0:T(8,128)S(1)} fusion(s32[2048,8]{1,0:T(8,128)S(1)} %dynamic-slice_bitcast_fusion.5, s32[1024]{0:T(1024)S(1)} %broadcast_clamp_fusion.2), kind=kCustom, calls=%fused_computation.1.clone.clone.1 | custom fusion | bytes 69632 | tf_op jit(solution)/shard_map/while/body/eval_jaxpr/jit(_take)/gather | solution.py:79
  111.0 1.3 fusion.23
  112.8 1.1 dynamic-slice_bitcast_fusion.4
  113.9 3.2 %gather_fusion = bf16[1024,128]{1,0:T(8,128)(2,1)S(1)} fusion(bf16[2048,128]{1,0:T(8,128)(2,1)S(1)} %dynamic-slice_bitcast_fusion.4, s32[1024]{0:T(1024)S(1)} %broadcast_clamp_fusion.2), kind=kCustom, calls=%fused_computation.clone.clone.1 | custom fusion | bytes 528384 | tf_op jit(solution)/shard_map/while/body/eval_jaxpr/jit(_take)/gather | solution.py:78
  117.6 1.3 dynamic-slice_bitcast_fusion.5
  120.3 2.8 %gather_fusion.1 = s32[1024,8]{1,0:T(8,128)S(1)} fusion(s32[2048,8]{1,0:T(8,128)S(1)} %dynamic-slice_bitcast_fusion.5, s32[1024]{0:T(1024)S(1)} %broadcast_clamp_fusion.2), kind=kCustom, calls=%fused_computation.1.clone.clone.1 | custom fusion | bytes 69632 | tf_op jit(solution)/shard_map/while/body/eval_jaxpr/jit(_take)/gather | solution.py:79
  123.1 1.3 fusion.23
  124.9 1.1 dynamic-slice_bitcast_fusion.4
  126.0 3.2 %gather_fusion = bf16[1024,128]{1,0:T(8,128)(2,1)S(1)} fusion(bf16[2048,128]{1,0:T(8,128)(2,1)S(1)} %dynamic-slice_bitcast_fusion.4, s32[1024]{0:T(1024)S(1)} %broadcast_clamp_fusion.2), kind=kCustom, calls=%fused_computation.clone.clone.1 | custom fusion | bytes 528384 | tf_op jit(solution)/shard_map/while/body/eval_jaxpr/jit(_take)/gather | solution.py:78
  129.7 1.3 dynamic-slice_bitcast_fusion.5
  132.3 2.8 %gather_fusion.1 = s32[1024,8]{1,0:T(8,128)S(1)} fusion(s32[2048,8]{1,0:T(8,128)S(1)} %dynamic-slice_bitcast_fusion.5, s32[1024]{0:T(1024)S(1)} %broadcast_clamp_fusion.2), kind=kCustom, calls=%fused_computation.1.clone.clone.1 | custom fusion | bytes 69632 | tf_op jit(solution)/shard_map/while/body/eval_jaxpr/jit(_take)/gather | solution.py:79
  135.1 1.3 fusion.23
  136.9 1.1 dynamic-slice_bitcast_fusion.4
  138.0 3.2 %gather_fusion = bf16[1024,128]{1,0:T(8,128)(2,1)S(1)} fusion(bf16[2048,128]{1,0:T(8,128)(2,1)S(1)} %dynamic-slice_bitcast_fusion.4, s32[1024]{0:T(1024)S(1)} %broadcast_clamp_fusion.2), kind=kCustom, calls=%fused_computation.clone.clone.1 | custom fusion | bytes 528384 | tf_op jit(solution)/shard_map/while/body/eval_jaxpr/jit(_take)/gather | solution.py:78
  141.7 1.3 dynamic-slice_bitcast_fusion.5
  144.4 2.8 %gather_fusion.1 = s32[1024,8]{1,0:T(8,128)S(1)} fusion(s32[2048,8]{1,0:T(8,128)S(1)} %dynamic-slice_bitcast_fusion.5, s32[1024]{0:T(1024)S(1)} %broadcast_clamp_fusion.2), kind=kCustom, calls=%fused_computation.1.clone.clone.1 | custom fusion | bytes 69632 | tf_op jit(solution)/shard_map/while/body/eval_jaxpr/jit(_take)/gather | solution.py:79
  147.2 1.3 fusion.23
  149.0 1.1 dynamic-slice_bitcast_fusion.4
  150.1 3.2 %gather_fusion = bf16[1024,128]{1,0:T(8,128)(2,1)S(1)} fusion(bf16[2048,128]{1,0:T(8,128)(2,1)S(1)} %dynamic-slice_bitcast_fusion.4, s32[1024]{0:T(1024)S(1)} %broadcast_clamp_fusion.2), kind=kCustom, calls=%fused_computation.clone.clone.1 | custom fusion | bytes 528384 | tf_op jit(solution)/shard_map/while/body/eval_jaxpr/jit(_take)/gather | solution.py:78
  153.8 1.3 dynamic-slice_bitcast_fusion.5
  156.4 2.8 %gather_fusion.1 = s32[1024,8]{1,0:T(8,128)S(1)} fusion(s32[2048,8]{1,0:T(8,128)S(1)} %dynamic-slice_bitcast_fusion.5, s32[1024]{0:T(1024)S(1)} %broadcast_clamp_fusion.2), kind=kCustom, calls=%fused_computation.1.clone.clone.1 | custom fusion | bytes 69632 | tf_op jit(solution)/shard_map/while/body/eval_jaxpr/jit(_take)/gather | solution.py:79
  159.2 1.3 fusion.23
  161.0 1.1 dynamic-slice_bitcast_fusion.4
  162.1 3.2 %gather_fusion = bf16[1024,128]{1,0:T(8,128)(2,1)S(1)} fusion(bf16[2048,128]{1,0:T(8,128)(2,1)S(1)} %dynamic-slice_bitcast_fusion.4, s32[1024]{0:T(1024)S(1)} %broadcast_clamp_fusion.2), kind=kCustom, calls=%fused_computation.clone.clone.1 | custom fusion | bytes 528384 | tf_op jit(solution)/shard_map/while/body/eval_jaxpr/jit(_take)/gather | solution.py:78
  165.8 1.3 dynamic-slice_bitcast_fusion.5
  168.5 2.8 %gather_fusion.1 = s32[1024,8]{1,0:T(8,128)S(1)} fusion(s32[2048,8]{1,0:T(8,128)S(1)} %dynamic-slice_bitcast_fusion.5, s32[1024]{0:T(1024)S(1)} %broadcast_clamp_fusion.2), kind=kCustom, calls=%fused_computation.1.clone.clone.1 | custom fusion | bytes 69632 | tf_op jit(solution)/shard_map/while/body/eval_jaxpr/jit(_take)/gather | solution.py:79
  171.3 1.3 fusion.23
  174.2 3.2 %gather_fusion = bf16[1024,128]{1,0:T(8,128)(2,1)S(1)} fusion(bf16[2048,128]{1,0:T(8,128)(2,1)S(1)} %dynamic-slice_bitcast_fusion.4, s32[1024]{0:T(1024)S(1)} %broadcast_clamp_fusion.2), kind=kCustom, calls=%fused_computation.clone.clone.1 | custom fusion | bytes 528384 | tf_op jit(solution)/shard_map/while/body/eval_jaxpr/jit(_take)/gather | solution.py:78
  177.9 1.3 dynamic-slice_bitcast_fusion.5
  180.5 2.8 %gather_fusion.1 = s32[1024,8]{1,0:T(8,128)S(1)} fusion(s32[2048,8]{1,0:T(8,128)S(1)} %dynamic-slice_bitcast_fusion.5, s32[1024]{0:T(1024)S(1)} %broadcast_clamp_fusion.2), kind=kCustom, calls=%fused_computation.1.clone.clone.1 | custom fusion | bytes 69632 | tf_op jit(solution)/shard_map/while/body/eval_jaxpr/jit(_take)/gather | solution.py:79
  183.3 1.3 fusion.23
  186.2 3.2 %gather_fusion = bf16[1024,128]{1,0:T(8,128)(2,1)S(1)} fusion(bf16[2048,128]{1,0:T(8,128)(2,1)S(1)} %dynamic-slice_bitcast_fusion.4, s32[1024]{0:T(1024)S(1)} %broadcast_clamp_fusion.2), kind=kCustom, calls=%fused_computation.clone.clone.1 | custom fusion | bytes 528384 | tf_op jit(solution)/shard_map/while/body/eval_jaxpr/jit(_take)/gather | solution.py:78
  190.7 3.3 %all-to-all-start.1 = ((s32[1,8,1024]{2,0,1:T(1,128)}), s32[1,8,1024]{2,0,1:T(1,128)S(1)}, u32[]{:S(2)}, u32[]{:S(2)}) async-start(s32[1,8,1024]{2,0,1:T(1,128)} %broadcast_in_dim.94), calls=%async_computation.1 | async-start | bytes 65536 | tf_op jit(solution)/shard_map/all_to_all | solution.py:101
  195.2 2.1 reduce.1
  198.3 3.4 %all-to-all-start = ((bf16[4,2,16384]{2,1,0:T(2,128)(2,1)}), bf16[4,2,16384]{2,1,0:T(2,128)(2,1)S(1)}, u32[]{:S(2)}, u32[]{:S(2)}) async-start(bf16[4,2,16384]{2,1,0:T(2,128)(2,1)} %reshape.97), calls=%async_computation | async-start | bytes 524288 | tf_op jit(solution)/shard_map/all_to_all | solution.py:100
  203.5 4.2 %all-to-all-done = bf16[4,2,16384]{2,1,0:T(2,128)(2,1)S(1)} async-done(((bf16[4,2,16384]{2,1,0:T(2,128)(2,1)}), bf16[4,2,16384]{2,1,0:T(2,128)(2,1)S(1)}, u32[]{:S(2)}, u32[]{:S(2)}) %all-to-all-start) | async-done | bytes 262176 | tf_op jit(solution)/shard_map/all_to_all | solution.py:100
  208.1 1.4 fusion.13
  209.4 1.4 fusion.14
  210.8 34.7 %all-reduce.2 = (f32[2,16,256]{2,1,0:T(8,128)S(1)}, f32[2,256]{1,0:T(2,128)S(1)}) all-reduce(f32[2,16,256]{2,1,0:T(8,128)S(1)} %pad_maximum_fusion, f32[2,256]{1,0:T(2,128)S(1)} %pad_maximum_fusion.1), channel_id=1, replica_groups=mesh['wide'=8,'sub'=4] {'wide'}, use_global_device_ids=true, to_apply=%region_5.6 | all-reduce | flops 8704 | bytes 69632 | tf_op jit(solution)/shard_map/psum | solution.py:116
  (102 shorter events, 36.6 us)
Async XLA Ops:
  7.2 186.8 %copy-start = (bf16[128,128]{1,0:T(8,128)(2,1)S(1)}, bf16[128,128]{1,0:T(8,128)(2,1)}, u32[]{:S(2)}) copy-start(bf16[128,128]{1,0:T(8,128)(2,1)} %param.11) | copy-start | bytes 98308
  7.2 86.3 %all-gather.3.cloned.1.call-start = ((), (), s32[]{:S(2)}) async-start(), calls=%async_computation.2 | async-start | bytes 4718592 | tf_op jit(solution)/shard_map/all_gather | solution.py:89
  7.9 45.9 %collective-permute-start = (s32[1,2048,8]{1,2,0:T(8,128)}, s32[1,2048,8]{1,2,0:T(8,128)S(1)}, u32[]{:S(2)}, u32[]{:S(2)}) collective-permute-start(s32[1,2048,8]{1,2,0:T(8,128)} %bitcast.58), channel_id=1, source_target_pairs={{0,4},{4,8},{8,12},{12,16},{16,20},{20,24},{24,28},{28,0},{1,5},{5... | collective-permute-start | bytes 196616 | tf_op jit(solution)/shard_map/ppermute | solution.py:24
  14.9 40.7 %collective-permute-start.1 = (s32[1,2048,8]{1,2,0:T(8,128)}, s32[1,2048,8]{1,2,0:T(8,128)S(1)}, u32[]{:S(2)}, u32[]{:S(2)}) collective-permute-start(s32[1,2048,8]{1,2,0:T(8,128)} %bitcast.59), channel_id=1, source_target_pairs={{0,28},{4,0},{8,4},{12,8},{16,12},{20,16},{24,20},{28,24},{1,29},{... | collective-permute-start | bytes 196616 | tf_op jit(solution)/shard_map/ppermute | solution.py:29
  54.2 9.0 %collective-permute-start.2 = (s32[1,2048,8]{1,2,0:T(8,128)S(1)}, s32[1,2048,8]{1,2,0:T(8,128)S(1)}, u32[]{:S(2)}, u32[]{:S(2)}) collective-permute-start(s32[1,2048,8]{1,2,0:T(8,128)S(1)} %collective-permute-done), channel_id=1, source_target_pairs={{0,4},{4,8},{8,12},{12,16},{16,20},{20,24},{24,28},{28,0},{1,5},{5... | collective-permute-start | bytes 196616 | tf_op jit(solution)/shard_map/ppermute | solution.py:24
  55.9 7.7 %collective-permute-start.3 = (s32[1,2048,8]{1,2,0:T(8,128)S(1)}, s32[1,2048,8]{1,2,0:T(8,128)S(1)}, u32[]{:S(2)}, u32[]{:S(2)}) collective-permute-start(s32[1,2048,8]{1,2,0:T(8,128)S(1)} %collective-permute-done.1), channel_id=1, source_target_pairs={{0,28},{4,0},{8,4},{12,8},{16,12},{20,16},{24,20},{28,24},{1,29},{... | collective-permute-start | bytes 196616 | tf_op jit(solution)/shard_map/ppermute | solution.py:29
  63.5 8.8 %collective-permute-start.4 = (s32[1,2048,8]{1,2,0:T(8,128)S(1)}, s32[1,2048,8]{1,2,0:T(8,128)S(1)}, u32[]{:S(2)}, u32[]{:S(2)}) collective-permute-start(s32[1,2048,8]{1,2,0:T(8,128)S(1)} %collective-permute-done.2), channel_id=1, source_target_pairs={{0,4},{4,8},{8,12},{12,16},{16,20},{20,24},{24,28},{28,0},{1,5},{5... | collective-permute-start | bytes 196616 | tf_op jit(solution)/shard_map/ppermute | solution.py:24
  63.9 8.8 %collective-permute-start.5 = (s32[1,2048,8]{1,2,0:T(8,128)S(1)}, s32[1,2048,8]{1,2,0:T(8,128)S(1)}, u32[]{:S(2)}, u32[]{:S(2)}) collective-permute-start(s32[1,2048,8]{1,2,0:T(8,128)S(1)} %collective-permute-done.3), channel_id=1, source_target_pairs={{0,28},{4,0},{8,4},{12,8},{16,12},{20,16},{24,20},{28,24},{1,29},{... | collective-permute-start | bytes 196616 | tf_op jit(solution)/shard_map/ppermute | solution.py:29
  72.6 7.0 %collective-permute-start.6 = (s32[1,2048,8]{1,2,0:T(8,128)S(1)}, s32[1,2048,8]{1,2,0:T(8,128)S(1)}, u32[]{:S(2)}, u32[]{:S(2)}) collective-permute-start(s32[1,2048,8]{1,2,0:T(8,128)S(1)} %collective-permute-done.4), channel_id=1, source_target_pairs={{0,4},{4,8},{8,12},{12,16},{16,20},{20,24},{24,28},{28,0},{1,5},{5... | collective-permute-start | bytes 196616 | tf_op jit(solution)/shard_map/ppermute | solution.py:24
  190.7 7.5 %all-to-all-start.1 = ((s32[1,8,1024]{2,0,1:T(1,128)}), s32[1,8,1024]{2,0,1:T(1,128)S(1)}, u32[]{:S(2)}, u32[]{:S(2)}) async-start(s32[1,8,1024]{2,0,1:T(1,128)} %broadcast_in_dim.94), calls=%async_computation.1 | async-start | bytes 65536 | tf_op jit(solution)/shard_map/all_to_all | solution.py:101
  198.3 9.4 %all-to-all-start = ((bf16[4,2,16384]{2,1,0:T(2,128)(2,1)}), bf16[4,2,16384]{2,1,0:T(2,128)(2,1)S(1)}, u32[]{:S(2)}, u32[]{:S(2)}) async-start(bf16[4,2,16384]{2,1,0:T(2,128)(2,1)} %reshape.97), calls=%async_computation | async-start | bytes 524288 | tf_op jit(solution)/shard_map/all_to_all | solution.py:100
  208.0 38.2 %copy-start.1 = (bf16[1,128,1024]{2,1,0:T(8,128)(2,1)}, bf16[1,128,1024]{2,1,0:T(8,128)(2,1)S(1)}, u32[]{:S(2)}) copy-start(bf16[1,128,1024]{2,1,0:T(8,128)(2,1)S(1)} %copy.28) | copy-start | bytes 786436
Sparse Core Ops, SparseCore 0:
  10.1 83.3 all-gather.2
